TPU v7x, 32 devices: a whole 2x2x4 slice. The times are simulated.
32 devices in a mesh: groups: 2 (over x), rows: 16 (over z, y, core).
Axes of the slice: x: 2, y: 2, z: 4, core: 2. Of those that a mesh axis runs over, the one named last changes fastest.
Arguments:
- context: bfloat16 [256, 256, 256], P(('groups', 'rows')), parts along dimension 0, may hold values from -6 to 6
- conv_weight: bfloat16 [3, 3, 256, 256], replicated, may hold values from -0.125 to 0.125
- conv_bias: float32 [256], replicated, may hold values from -3 to 3
- hr_features: bfloat16 [512, 512, 256], P(('groups', 'rows')), parts along dimension 0, may hold values from -6 to 6
- proj_weight: bfloat16 [512, 256], replicated, may hold values from -0.25 to 0.25
- cot_joined: bfloat16 [512, 512, 256], P(('groups', 'rows')), parts along dimension 0, may hold values from -6 to 6
- cot_context: bfloat16 [256, 256, 256], P(('groups', 'rows')), parts along dimension 0, may hold values from -6 to 6
Outputs:
- joined: bfloat16 [512, 512, 256], P(('groups', 'rows')), parts along dimension 0
- grad_context: float32 [256, 256, 256], P(('groups', 'rows')), parts along dimension 0
- grad_conv_weight: float32 [6, 3, 256, 256], P('groups'), parts along dimension 0
- grad_conv_bias: float32 [512], P('groups'), parts along dimension 0
- grad_proj_weight: float32 [1024, 256], P('groups'), parts along dimension 0
There are 2 independent parts, one for each index of `groups`. A program takes and returns all parts, laid end to end along the dimension named above; an argument that names none is the same for every part. Nothing has to cross between parts.
All inputs are finite; a program needn't handle non-finite values.
Results may differ from a plain program's by a relative error of at most 0.0053.
Values may be sent and summed in bfloat16 or wider, within the bound.
A program may use at most 128 MiB of HBM per device.

v0:
```python
import functools

import jax
import jax.numpy as jnp
from jax import lax
from jax.experimental import pallas as pl
from jax.experimental.pallas import tpu as pltpu
from jax.sharding import PartitionSpec as P

MESH = pl.DeviceIdType.MESH
BF = jnp.bfloat16
F32 = jnp.float32
VMEM_LIMIT = 56 * 1024 * 1024


def dot(lhs, rhs):
    return jnp.dot(lhs, rhs, preferred_element_type=F32)


def dot_t(lhs, rhs):
    return lax.dot_general(lhs, rhs, (((1,), (1,)), ((), ())), preferred_element_type=F32)


def t_dot(lhs, rhs):
    return lax.dot_general(lhs, rhs, (((0,), (0,)), ((), ())), preferred_element_type=F32)


def sigmoid(values):
    return 0.5 * jnp.tanh(0.5 * values) + 0.5


def enter(size):
    group, me = lax.axis_index("groups"), lax.axis_index("rows")
    barrier = pltpu.get_barrier_semaphore()

    def greet(step, carry):
        peer = lax.rem(me + step, size)
        pl.semaphore_signal(barrier, inc=1, device_id=(group, peer), device_id_type=MESH)
        return carry

    lax.fori_loop(1, size, greet, 0)
    pl.semaphore_wait(barrier, size - 1)
    return group, me


def gather_kernel(size, left, width, ctx, cot, c_top, c_bot, g_top, g_bot, crop, send, recv, local):
    group, me = enter(size)
    rows = ctx.shape[0]
    units = rows // 2
    base = 3 * size // 2

    def remote(src, dst, number, slot, peer):
        return pltpu.make_async_remote_copy(
            src_ref=src,
            dst_ref=dst,
            send_sem=send.at[number],
            recv_sem=recv.at[slot],
            device_id=(group, peer),
            device_id_type=MESH,
        )

    def unit(j):
        return ctx.at[pl.ds(2 * j, 2), pl.ds(left, width)]

    def place(k):
        return crop.at[pl.ds(2 * k, 2)]

    sends = []
    for j in range(units):
        index = units * me + j - base
        for k, ok, target in (
            (1, (index >= 0) & (index < size), index),
            (0, index == -1, 0),
            (2, index == size, size - 1),
        ):
            if j != units - 1 and k == 0:
                continue
            if j != 0 and k == 2:
                continue
            copy = remote(unit(j), place(k), len(sends), k, target)
            far = ok & (target != me)
            sends.append((far, copy))
            pl.when(far)(copy.start)
            if k == 1:
                near = pltpu.make_async_copy(unit(j), place(1), local)

                @pl.when(ok & (target == me))
                def _():
                    near.start()
                    near.wait()

    has_up, has_down = me > 0, me < size - 1
    for ok, peer, src, dst, slot in (
        (has_up, me - 1, ctx.at[pl.ds(0, 2)], c_bot, 3),
        (has_down, me + 1, ctx.at[pl.ds(rows - 2, 2)], c_top, 4),
        (has_up, me - 1, cot.at[pl.ds(0, 1)], g_bot, 5),
        (has_down, me + 1, cot.at[pl.ds(rows - 1, 1)], g_top, 6),
    ):
        copy = remote(src, dst, len(sends), slot, peer)
        sends.append((ok, copy))
        pl.when(ok)(copy.start)

    @pl.when(me == 0)
    def _():
        c_top[...] = jnp.zeros_like(c_top)
        g_top[...] = jnp.zeros_like(g_top)

    @pl.when(me == size - 1)
    def _():
        c_bot[...] = jnp.zeros_like(c_bot)
        g_bot[...] = jnp.zeros_like(g_bot)

    mine = (base + me) // units
    take = remote(place(1), place(1), 0, 1, me)
    pl.when(mine != me)(take.wait_recv)
    for ok, peer, k in ((has_up, me - 1, 2), (has_down, me + 1, 0)):
        copy = remote(place(1), place(k), len(sends), k, peer)
        sends.append((ok, copy))
        pl.when(ok)(copy.start)
    for k in (0, 2):
        remote(place(k), place(k), 0, k, me).wait_recv()
    pl.when(has_up)(remote(c_top, c_top, 0, 4, me).wait_recv)
    pl.when(has_up)(remote(g_top, g_top, 0, 6, me).wait_recv)
    pl.when(has_down)(remote(c_bot, c_bot, 0, 3, me).wait_recv)
    pl.when(has_down)(remote(g_bot, g_bot, 0, 5, me).wait_recv)
    for ok, copy in sends:
        pl.when(ok)(copy.wait_send)


def gather(size, context, cot_context, left, width):
    rows, cols, channels = context.shape
    shapes = [(2, cols, channels)] * 2 + [(1, cols, channels)] * 2 + [(6, width, channels)]
    return pl.pallas_call(
        functools.partial(gather_kernel, size, left, width),
        out_shape=[jax.ShapeDtypeStruct(shape, BF) for shape in shapes],
        in_specs=[pl.BlockSpec(memory_space=pl.ANY)] * 2,
        out_specs=[pl.BlockSpec(memory_space=pltpu.VMEM)] * 5,
        scratch_shapes=[
            pltpu.SemaphoreType.DMA((rows // 2 + 8,)),
            pltpu.SemaphoreType.DMA((7,)),
            pltpu.SemaphoreType.DMA,
        ],
        compiler_params=pltpu.CompilerParams(
            collective_id=0, has_side_effects=True, vmem_limit_bytes=VMEM_LIMIT
        ),
    )(context, cot_context)


def fine_kernel(
    size, lead, crop_ctx, conv_w, bias, proj, blend, blend_t, hr, cot,
    joined, wgrad, parts, crop, upper, acc,
):
    step = pl.program_id(0)
    me = lax.axis_index("rows")
    channels = hr.shape[2]
    cols = hr.shape[1]
    narrow, wide = blend.shape[1], crop_ctx.shape[1]
    chunk = 128

    @pl.when(step == 0)
    def _():
        shifted = []
        for b in range(3):
            total = None
            for a in range(3):
                rows = crop_ctx[pl.ds(a, 4)].reshape(4 * wide, channels)
                term = dot(rows, conv_w[a, b])
                total = term if total is None else total + term
            shifted.append(total.reshape(4, wide, channels))
        for row in range(4):
            pre = bias[...] + sum(
                shifted[b][row, lead + b - 1 : lead + b - 1 + narrow] for b in range(3)
            )
            value = crop_ctx[row + 1, lead : lead + narrow].astype(F32) + pre * sigmoid(pre)
            crop[row] = value.astype(BF)

        @pl.when(me == 0)
        def _():
            crop[0] = crop[1]

        @pl.when(me == size - 1)
        def _():
            crop[3] = crop[2]

        for row in range(4):
            coarse = dot(crop[row], proj[pl.ds(channels, channels)]).astype(BF)
            upper[row] = dot(blend[...], coarse)
        acc[...] = jnp.zeros_like(acc)
        wgrad[...] = jnp.zeros_like(wgrad)

    low = (step + 1) // 2
    start = jnp.where(step % 2 == 0, 9, 1)
    weights = [(2 * k + start).astype(F32) * (1.0 / 16.0) for k in range(4)]

    def body(c, carry):
        at = pl.ds(pl.multiple_of(c * chunk, chunk), chunk)
        lo, hi = upper[low, at], upper[low + 1, at]
        x = hr[:, at].reshape(4 * chunk, channels)
        base = dot(x, proj[pl.ds(0, channels)])
        grads = []
        first = second = None
        for k in range(4):
            v = base[k * chunk : (k + 1) * chunk] + (lo + weights[k] * (hi - lo))
            s = sigmoid(v)
            j = v * s
            joined[k, at] = j.astype(BF)
            g = (cot[k, at].astype(F32) * (s + j * (1.0 - s))).astype(BF)
            grads.append(g)
            g = g.astype(F32)
            part = weights[k] * g
            second = part if second is None else second + part
            rest = g - part
            first = rest if first is None else first + rest
        acc[low, at] += first
        acc[low + 1, at] += second
        wgrad[pl.ds(0, channels)] += t_dot(x, jnp.concatenate(grads, axis=0))
        return carry

    lax.fori_loop(0, cols // chunk, body, 0)

    @pl.when(step == pl.num_programs(0) - 1)
    def _():
        back = [dot(blend_t[...], acc[row].astype(BF)) for row in range(4)]
        top = jnp.where(me == 0, 1.0, 0.0)
        bottom = jnp.where(me == size - 1, 1.0, 0.0)
        back[1] = back[1] + top * back[0]
        back[2] = back[2] + bottom * back[3]
        back = [back[0] * (1.0 - top), back[1], back[2], back[3] * (1.0 - bottom)]
        bottom_w = proj[pl.ds(channels, channels)]
        total = None
        for row in range(4):
            low_back = back[row].astype(BF)
            parts[row] = dot_t(low_back, bottom_w)
            term = t_dot(crop[row], low_back)
            total = term if total is None else total + term
        wgrad[pl.ds(channels, channels)] = total


def fine(size, lead, crop_ctx, conv_weight, conv_bias, proj_weight, hr, cot):
    fine_rows, cols, channels = hr.shape
    narrow = cols // 8
    index = 2 * jnp.arange(cols, dtype=jnp.int32) - 7
    lower = jnp.floor_divide(index, 16)
    frac = (index - 16 * lower).astype(F32) / 16.0
    column = jnp.arange(narrow, dtype=jnp.int32)[None, :]
    left = jnp.clip(lower, 0, narrow - 1)[:, None]
    right = jnp.clip(lower + 1, 0, narrow - 1)[:, None]
    blend = (1.0 - frac)[:, None] * (column == left).astype(F32)
    blend = (blend + frac[:, None] * (column == right).astype(F32)).astype(BF)
    whole = lambda shape: pl.BlockSpec(shape, lambda s: (0,) * len(shape))
    tile = pl.BlockSpec((4, cols, channels), lambda s: (s, 0, 0))
    return pl.pallas_call(
        functools.partial(fine_kernel, size, lead),
        grid=(fine_rows // 4,),
        out_shape=[
            jax.ShapeDtypeStruct(hr.shape, BF),
            jax.ShapeDtypeStruct((2 * channels, channels), F32),
            jax.ShapeDtypeStruct((4, narrow, channels), F32),
        ],
        in_specs=[
            whole(crop_ctx.shape),
            whole(conv_weight.shape),
            whole((1, channels)),
            whole(proj_weight.shape),
            whole((cols, narrow)),
            whole((narrow, cols)),
            tile,
            tile,
        ],
        out_specs=[tile, whole((2 * channels, channels)), whole((4, narrow, channels))],
        scratch_shapes=[
            pltpu.VMEM((4, narrow, channels), BF),
            pltpu.VMEM((4, cols, channels), F32),
            pltpu.VMEM((4, cols, channels), F32),
        ],
        compiler_params=pltpu.CompilerParams(vmem_limit_bytes=VMEM_LIMIT),
    )(crop_ctx, conv_weight, conv_bias.reshape(1, -1), proj_weight, blend, blend.T, hr, cot)


def scatter_kernel(size, units, parts, out, up, down, got_up, got_down, mine, send, recv, edge):
    group, me = enter(size)
    base = 3 * size // 2

    def remote(src, dst, s, r, peer):
        return pltpu.make_async_remote_copy(
            src_ref=src,
            dst_ref=dst,
            send_sem=s,
            recv_sem=r,
            device_id=(group, peer),
            device_id_type=MESH,
        )

    has_up, has_down = me > 0, me < size - 1
    up[...] = parts[0].astype(BF)
    down[...] = parts[3].astype(BF)
    to_up = remote(up, got_down, send.at[0], edge.at[0], me - 1)
    to_down = remote(down, got_up, send.at[1], edge.at[1], me + 1)
    pl.when(has_up)(to_up.start)
    pl.when(has_down)(to_down.start)

    @pl.when(me == 0)
    def _():
        got_up[...] = jnp.zeros_like(got_up)

    @pl.when(me == size - 1)
    def _():
        got_down[...] = jnp.zeros_like(got_down)

    for s in range(units + 2):
        index = units * me + s - 1 - base

        @pl.when((index < 0) | (index >= size))
        def _():
            out[s] = jnp.zeros_like(out[s])

    pl.when(has_up)(remote(got_up, got_up, send.at[0], edge.at[1], me).wait_recv)
    pl.when(has_down)(remote(got_down, got_down, send.at[0], edge.at[0], me).wait_recv)
    mine[0] = (parts[1] + got_up[...].astype(F32)).astype(BF)
    mine[1] = (parts[2] + got_down[...].astype(F32)).astype(BF)
    number = base + me
    waits = []
    for s in range(units + 2):
        offset = number + 1 - s
        owner = offset // units
        ok = lax.rem(offset, units) == 0
        copy = remote(mine, out.at[s], send.at[2 + s], recv.at[s], owner)
        far = ok & (owner != me) & (owner >= 0) & (owner < size)
        waits.append((far, copy))
        pl.when(far)(copy.start)

        @pl.when(ok & (owner == me))
        def _():
            out[s] = mine[...]

    for s in range(units + 2):
        index = units * me + s - 1 - base
        here = (index >= 0) & (index < size) & (index != me)
        pl.when(here)(remote(mine, out.at[s], send.at[0], recv.at[s], me).wait_recv)
    for far, copy in waits:
        pl.when(far)(copy.wait_send)
    pl.when(has_up)(to_up.wait_send)
    pl.when(has_down)(to_down.wait_send)


def scatter(size, units, parts):
    _, narrow, channels = parts.shape
    row = (narrow, channels)
    return pl.pallas_call(
        functools.partial(scatter_kernel, size, units),
        out_shape=jax.ShapeDtypeStruct((units + 2, 2) + row, BF),
        in_specs=[pl.BlockSpec(memory_space=pltpu.VMEM)],
        out_specs=pl.BlockSpec(memory_space=pltpu.VMEM),
        scratch_shapes=[pltpu.VMEM(row, BF)] * 4
        + [
            pltpu.VMEM((2,) + row, BF),
            pltpu.SemaphoreType.DMA((units + 4,)),
            pltpu.SemaphoreType.DMA((units + 2,)),
            pltpu.SemaphoreType.DMA((2,)),
        ],
        compiler_params=pltpu.CompilerParams(
            collective_id=1, has_side_effects=True, vmem_limit_bytes=VMEM_LIMIT
        ),
    )(parts)


def coarse_kernel(
    left, ctx, c_top, c_bot, cot, g_top, g_bot, crop_grad, conv_w, bias,
    grad, wgrad, bgrad, ext, ext_t, outg, pre_g,
):
    rows, cols, channels = ctx.shape
    narrow = crop_grad.shape[1]
    ext[pl.ds(0, 2)] = c_top[...]
    ext[pl.ds(2, rows)] = ctx[...]
    ext[pl.ds(rows + 2, 2)] = c_bot[...]
    outg[pl.ds(0, 1)] = g_top[...].astype(F32)
    outg[pl.ds(1, rows)] = cot[...].astype(F32)
    outg[pl.ds(rows + 1, 1)] = g_bot[...].astype(F32)
    for r in range(rows + 2):
        outg[r, pl.ds(left, narrow)] += crop_grad[r + 1].astype(F32)
    column = lax.broadcasted_iota(jnp.int32, (cols, channels), 0)

    def later(v):
        return jnp.where(column == 0, 0.0, pltpu.roll(v, 1, 0))

    def sooner(v):
        return jnp.where(column == cols - 1, 0.0, pltpu.roll(v, cols - 1, 0))

    def turn(r, carry):
        ext_t[r] = jnp.transpose(ext[r + 1])
        return carry

    lax.fori_loop(0, rows + 2, turn, 0)
    bgrad[...] = jnp.zeros_like(bgrad)

    def forward(p, carry):
        sums = []
        for b in range(3):
            total = None
            for a in range(3):
                term = dot(ext[pl.ds(2 * p + a, 2)].reshape(2 * cols, channels), conv_w[a, b])
                total = term if total is None else total + term
            sums.append(total)
        for k in range(2):
            cut = slice(k * cols, (k + 1) * cols)
            r = 2 * p + k
            v = bias[...] + later(sums[0][cut]) + sums[1][cut] + sooner(sums[2][cut])
            s = sigmoid(v)
            g = (outg[r] * (s * (1.0 + v * (1.0 - s)))).astype(BF)
            pre_g[1, r] = g
            g = g.astype(F32)
            pre_g[0, r] = sooner(g).astype(BF)
            pre_g[2, r] = later(g).astype(BF)
            own = ((r >= 1) & (r <= rows)).astype(F32)
            bgrad[...] += own * jnp.sum(g, axis=0, keepdims=True)
        return carry

    lax.fori_loop(0, (rows + 2) // 2, forward, 0)

    def backward(p, carry):
        sums = []
        for b in range(3):
            total = None
            for a in range(3):
                term = dot_t(
                    pre_g[1, pl.ds(2 * p + 2 - a, 2)].reshape(2 * cols, channels), conv_w[a, b]
                )
                total = term if total is None else total + term
            sums.append(total)
        for k in range(2):
            cut = slice(k * cols, (k + 1) * cols)
            r = 2 * p + k
            grad[r] = outg[r + 1] + (sooner(sums[0][cut]) + sums[1][cut] + later(sums[2][cut]))
        return carry

    lax.fori_loop(0, rows // 2, backward, 0)

    def weights(n, carry):
        a, b = n // 3, n % 3
        total = None
        for i in range(rows):
            term = dot(ext_t[i + a], pre_g[b, i + 1])
            total = term if total is None else total + term
        wgrad[n] = total
        return carry

    lax.fori_loop(0, 9, weights, 0)


def coarse(left, context, halos, cot_context, crop_grad, conv_weight, conv_bias):
    rows, cols, channels = context.shape
    c_top, c_bot, g_top, g_bot = halos
    return pl.pallas_call(
        functools.partial(coarse_kernel, left),
        out_shape=[
            jax.ShapeDtypeStruct((rows, cols, channels), F32),
            jax.ShapeDtypeStruct((9, channels, channels), F32),
            jax.ShapeDtypeStruct((1, channels), F32),
        ],
        in_specs=[pl.BlockSpec(memory_space=pltpu.VMEM)] * 9,
        out_specs=[pl.BlockSpec(memory_space=pltpu.VMEM)] * 3,
        scratch_shapes=[
            pltpu.VMEM((rows + 4, cols, channels), BF),
            pltpu.VMEM((rows + 2, channels, cols), BF),
            pltpu.VMEM((rows + 2, cols, channels), F32),
            pltpu.VMEM((3, rows + 2, cols, channels), BF),
        ],
        compiler_params=pltpu.CompilerParams(vmem_limit_bytes=VMEM_LIMIT),
    )(context, c_top, c_bot, cot_context, g_top, g_bot, crop_grad, conv_weight,
      conv_bias.reshape(1, -1))


def per_device(size, context, conv_weight, conv_bias, hr_features, proj_weight, cot_joined,
               cot_context):
    rows, cols, channels = context.shape
    narrow = hr_features.shape[1] // 8
    left = (cols - narrow) // 2
    lead = 16
    *halos, crop_ctx = gather(size, context, cot_context, left - lead, narrow + 2 * lead)
    joined, proj_grad, parts = fine(
        size, lead, crop_ctx, conv_weight, conv_bias, proj_weight, hr_features, cot_joined
    )
    crop_grad = scatter(size, rows // 2, parts).reshape(-1, narrow, channels)
    grad, conv_grad, bias_grad = coarse(
        left, context, halos, cot_context, crop_grad, conv_weight, conv_bias
    )
    conv_grad, bias_grad, proj_grad = lax.psum((conv_grad, bias_grad, proj_grad), "rows")
    return (
        joined,
        grad,
        conv_grad.reshape(3, 3, channels, channels),
        bias_grad.reshape(-1),
        proj_grad,
    )


def solution(mesh):
    tile = P(("groups", "rows"), None, None)
    return jax.shard_map(
        functools.partial(per_device, mesh.shape["rows"]),
        mesh=mesh,
        in_specs=(tile, P(), P(), tile, P(), tile, tile),
        out_specs=(tile, tile, P("groups", None, None, None), P("groups"), P("groups", None)),
        check_vma=False,
    )
```

profile of v0, /device:TPU:0, one launch (start us, length us, event | category | flops | bytes accessed | tf_op | source)
XLA Modules:
  0.0 189.3 jit_solution(8407784382158354145)
XLA Ops:
  7.2 0.0 all-reduce.3.cloned.1.call-start
  7.2 0.7 add_convert_fusion.1.blend_t
  7.9 1.0 add_convert_fusion.blend
  8.9 12.4 %shard_map.110 = (bf16[2,256,256]{2,1,0:T(8,128)(2,1)}, bf16[2,256,256]{2,1,0:T(8,128)(2,1)}, bf16[1,256,256]{2,1,0:T(8,128)(2,1)}, bf16[1,256,256]{2,1,0:T(8,128)(2,1)}, bf16[6,96,256]{2,1,0:T(8,128)(2,1)}) custom-call(bf16[8,256,256]{2,1,0:T(8,128)(2,1)} %ctx.3, bf16[8,256,256]{2,1,0:T(8,128)(2,1)} %cot.5), custom_call_target="tpu_custom_call" | custom-call | tf_op jit(solution)/shard_map/pallas_call | solution.py:133
  21.3 16.6 %shard_map.111 = (bf16[16,512,256]{2,1,0:T(8,128)(2,1)}, f32[512,256]{1,0:T(8,128)}, f32[4,64,256]{2,1,0:T(8,128)}) custom-call(bf16[6,96,256]{2,1,0:T(8,128)(2,1)} %get-tuple-element.16.crop_ctx, bf16[3,3,256,256]{3,2,1,0:T(8,128)(2,1)} %conv_w.3, f32[1,256]{1,0:T(1,128)} %bitcast.6, bf16[512,256]{1,0:T(8,128)(2,1)} %proj.1, ...), custom_call_target="tpu_custom_call" | custom-call | tf_op jit(solution)/shard_map/pallas_call | solution.py:252
  37.9 17.1 %shard_map.112 = bf16[6,2,64,256]{3,2,1,0:T(8,128)(2,1)} custom-call(f32[4,64,256]{2,1,0:T(8,128)} %get-tuple-element.22.parts), custom_call_target="tpu_custom_call" | custom-call | tf_op jit(solution)/shard_map/pallas_call | solution.py:349
  54.9 17.7 %shard_map.113 = (f32[8,256,256]{2,1,0:T(8,128)}, f32[9,256,256]{2,1,0:T(8,128)}, f32[1,256]{1,0:T(1,128)}) custom-call(bf16[8,256,256]{2,1,0:T(8,128)(2,1)} %ctx.3, bf16[2,256,256]{2,1,0:T(8,128)(2,1)} %get-tuple-element.18.c_top, bf16[2,256,256]{2,1,0:T(8,128)(2,1)} %get-tuple-element.19.c_bot, bf16[8,256,256]{2,1,0:T(8,128)(2,1)} %cot.5, ...), custom_call_target="tpu_custom_call" | custom-call | tf_op jit(solution)/shard_map/pallas_call | solution.py:453
  72.6 0.0 copy-start.1
  72.6 0.0 all-reduce.3.cloned.1.call-update
  72.6 0.7 copy-done.1
  73.3 31.8 %psum.22 = f32[256]{0:T(256)} all-reduce(f32[256]{0:T(256)S(1)} %bitcast.8), channel_id=1, replica_groups=mesh['groups'=2,'rows'=16] {'rows'}, use_global_device_ids=true, to_apply=%region_1.2 | all-reduce | flops 256 | bytes 2048 | tf_op jit(solution)/shard_map/psum | solution.py:487
  105.1 73.2 %all-reduce.3.cloned.1.call-done = (f32[3,3,256,256]{3,2,1,0:T(8,128)}, f32[512,256]{1,0:T(8,128)}) async-done(((f32[3,3,256,256]{3,2,1,0:T(8,128)}, f32[512,256]{1,0:T(8,128)}), (f32[3,3,256,256]{3,2,1,0:T(8,128)}, f32[512,256]{1,0:T(8,128)})) %all-reduce.3.cloned.1.call-update) | async-done | bytes 2883600 | tf_op jit(solution)/shard_map/psum | solution.py:487
  178.3 0.0 copy-start
  178.3 3.3 %copy.14 = f32[3,3,256,256]{3,2,1,0:T(8,128)} copy(f32[3,3,256,256]{3,2,1,0:T(8,128)} %get-tuple-element.35) | data formatting | bytes 4718592
  181.6 0.0 copy-done
  181.6 0.8 copy.15
  (2 shorter events, 0.0 us)
Async XLA Ops:
  7.2 171.2 %all-reduce.3.cloned.1.call-start = ((), (), s32[]{:S(2)}) async-start(), calls=%async_computation | async-start | bytes 5767168 | tf_op jit(solution)/shard_map/psum | solution.py:487
  72.6 0.7 copy-start.1
  178.3 3.3 %copy-start = (f32[512,256]{1,0:T(8,128)S(1)}, f32[512,256]{1,0:T(8,128)}, u32[]{:S(2)}) copy-start(f32[512,256]{1,0:T(8,128)} %get-tuple-element.37) | copy-start | bytes 1572868
Sparse Core Ops, SparseCore 0:
  72.7 105.5 all-reduce.2
where the time goes:
time: 189 us
  waiting for transfers between devices  73.3 us (39%)
  Pallas kernels  63.7 us (34%)
  blocking collectives  31.8 us (17%)
  between operations  14.1 us (7%)
  local copies, waits for them, and re-layouts  4.73 us (3%)
    psum x1, waiting for transfers between devices, per_device(): lax.psum((conv_grad, bias_grad, proj_grad), 'rows')  73.2 us
    psum x1, blocking collectives, per_device(): lax.psum((conv_grad, bias_grad, proj_grad), 'rows')  31.8 us
    pallas_call x1, Pallas kernels, coarse(): pl.pallas_call(functools.partial(coarse_kernel, left), out_shape=[jax.Sha...  17.7 us
    pallas_call x1, Pallas kernels, scatter(): pl.pallas_call(functools.partial(scatter_kernel, size, units), out_shape=...  17.1 us
    pallas_call x1, Pallas kernels, fine(): pl.pallas_call(functools.partial(fine_kernel, size, lead), grid=(fine_row...  16.6 us
    pallas_call x1, Pallas kernels, gather(): pl.pallas_call(functools.partial(gather_kernel, size, left, width), out_s...  12.4 us
    unnamed x6, local copies, waits for them, and re-layouts  4.73 us
  transfers between devices with their start and end apart: 1, of which 1 were waited for; matrix products, arithmetic and copies ran while one was open for 0% of the time, Pallas kernels for 0%

commit v1 on v0

--- a/solution.py
+++ b/solution.py
@@ -412,7 +412,7 @@
             pre_g[0, r] = sooner(g).astype(BF)
             pre_g[2, r] = later(g).astype(BF)
             own = ((r >= 1) & (r <= rows)).astype(F32)
-            bgrad[...] += own * jnp.sum(g, axis=0, keepdims=True)
+            bgrad[pl.ds(0, 1)] += own * jnp.sum(g, axis=0, keepdims=True)
         return carry
 
     lax.fori_loop(0, (rows + 2) // 2, forward, 0)
@@ -455,7 +455,7 @@
         out_shape=[
             jax.ShapeDtypeStruct((rows, cols, channels), F32),
             jax.ShapeDtypeStruct((9, channels, channels), F32),
-            jax.ShapeDtypeStruct((1, channels), F32),
+            jax.ShapeDtypeStruct((8, channels), F32),
         ],
         in_specs=[pl.BlockSpec(memory_space=pltpu.VMEM)] * 9,
         out_specs=[pl.BlockSpec(memory_space=pltpu.VMEM)] * 3,
@@ -468,6 +468,140 @@
         compiler_params=pltpu.CompilerParams(vmem_limit_bytes=VMEM_LIMIT),
     )(context, c_top, c_bot, cot_context, g_top, g_bot, crop_grad, conv_weight,
       conv_bias.reshape(1, -1))
+
+
+def reduce_kernel(size, conv, proj, bias, out, acc, outgoing, incoming, send, recv, back, load):
+    group, me = lax.axis_index("groups"), lax.axis_index("rows")
+    total_rows, channels = acc.shape
+    half = channels // 2
+    bits = [2**k for k in range(size.bit_length() - 1)]
+    orders = (bits, bits[:1] + bits[2:] + bits[1:2])
+    steps = len(bits)
+    n_conv, n_proj, n_bias = conv.shape[0], proj.shape[0], bias.shape[0]
+    loads = [
+        pltpu.make_async_copy(conv, acc.at[pl.ds(0, n_conv)], load.at[0]),
+        pltpu.make_async_copy(proj, acc.at[pl.ds(n_conv, n_proj)], load.at[1]),
+        pltpu.make_async_copy(bias, acc.at[pl.ds(n_conv + n_proj, n_bias)], load.at[2]),
+    ]
+    for copy in loads:
+        copy.start()
+    used = n_conv + n_proj + n_bias
+    acc[pl.ds(used, total_rows - used)] = jnp.zeros((total_rows - used, channels), F32)
+
+    def side(bit):
+        return lax.rem(me // bit, 2)
+
+    def partner(bit):
+        return me + bit * (1 - 2 * side(bit))
+
+    barrier = pltpu.get_barrier_semaphore()
+    for bit in bits:
+        pl.semaphore_signal(barrier, inc=1, device_id=(group, partner(bit)), device_id_type=MESH)
+    pl.semaphore_wait(barrier, steps)
+    for copy in loads:
+        copy.wait()
+
+    def remote(src, dst, s, r, bit):
+        return pltpu.make_async_remote_copy(
+            src_ref=src,
+            dst_ref=dst,
+            send_sem=s,
+            recv_sem=r,
+            device_id=(group, partner(bit)),
+            device_id_type=MESH,
+        )
+
+    def rows_at(start, count):
+        return pl.ds(pl.multiple_of(start, 16), count)
+
+    low = [0, 0]
+    kept = [[], []]
+    copies = []
+    pending = [None, None]
+    for step in range(steps + 1):
+        for h in range(2):
+            lanes = pl.ds(h * half, half)
+            if step > 0:
+                count = total_rows >> step
+                pending[h].wait_recv()
+                got = incoming[pl.ds(total_rows - 2 * count, count), lanes]
+                acc[rows_at(low[h], count), lanes] += got.astype(F32)
+            if step < steps:
+                bit = orders[h][step]
+                count = total_rows >> (step + 1)
+                mine = low[h] + side(bit) * count
+                other = low[h] + (1 - side(bit)) * count
+                there = rows_at(other, count)
+                outgoing[there, lanes] = acc[there, lanes].astype(BF)
+                copy = remote(
+                    outgoing.at[there, lanes],
+                    incoming.at[pl.ds(total_rows - 2 * count, count), lanes],
+                    send.at[h, step],
+                    recv.at[h, step],
+                    bit,
+                )
+                copy.start()
+                copies.append(copy)
+                pending[h] = copy
+                low[h] = mine
+                kept[h].append(mine)
+            else:
+                here = rows_at(low[h], total_rows >> steps)
+                out[here, lanes] = acc[here, lanes].astype(BF)
+                bit = orders[h][steps - 1]
+                copy = remote(
+                    out.at[here, lanes],
+                    out.at[here, lanes],
+                    send.at[h, steps],
+                    back.at[h, steps - 1],
+                    bit,
+                )
+                copy.start()
+                copies.append(copy)
+                pending[h] = copy
+    for step in reversed(range(steps)):
+        for h in range(2):
+            lanes = pl.ds(h * half, half)
+            pending[h].wait_recv()
+            if step > 0:
+                here = rows_at(kept[h][step - 1], total_rows >> step)
+                copy = remote(
+                    out.at[here, lanes],
+                    out.at[here, lanes],
+                    send.at[h, 2 * steps - step],
+                    back.at[h, step - 1],
+                    orders[h][step - 1],
+                )
+                copy.start()
+                copies.append(copy)
+                pending[h] = copy
+    for copy in copies:
+        copy.wait_send()
+
+
+def reduce_sums(size, conv, proj, bias):
+    channels = conv.shape[1]
+    rows = conv.shape[0] + proj.shape[0] + bias.shape[0]
+    rows = -(-rows // (16 * size)) * 16 * size
+    steps = size.bit_length() - 1
+    return pl.pallas_call(
+        functools.partial(reduce_kernel, size),
+        out_shape=jax.ShapeDtypeStruct((rows, channels), BF),
+        in_specs=[pl.BlockSpec(memory_space=pl.ANY)] * 3,
+        out_specs=pl.BlockSpec(memory_space=pltpu.VMEM),
+        scratch_shapes=[
+            pltpu.VMEM((rows, channels), F32),
+            pltpu.VMEM((rows, channels), BF),
+            pltpu.VMEM((rows, channels), BF),
+            pltpu.SemaphoreType.DMA((2, 2 * steps)),
+            pltpu.SemaphoreType.DMA((2, steps)),
+            pltpu.SemaphoreType.DMA((2, steps)),
+            pltpu.SemaphoreType.DMA((3,)),
+        ],
+        compiler_params=pltpu.CompilerParams(
+            collective_id=2, has_side_effects=True, vmem_limit_bytes=VMEM_LIMIT
+        ),
+    )(conv, proj, bias)
 
 
 def per_device(size, context, conv_weight, conv_bias, hr_features, proj_weight, cot_joined,
@@ -484,13 +618,14 @@
     grad, conv_grad, bias_grad = coarse(
         left, context, halos, cot_context, crop_grad, conv_weight, conv_bias
     )
-    conv_grad, bias_grad, proj_grad = lax.psum((conv_grad, bias_grad, proj_grad), "rows")
+    sums = reduce_sums(size, conv_grad.reshape(-1, channels), proj_grad, bias_grad).astype(F32)
+    first, second = 9 * channels, 11 * channels
     return (
         joined,
         grad,
-        conv_grad.reshape(3, 3, channels, channels),
-        bias_grad.reshape(-1),
-        proj_grad,
+        sums[:first].reshape(3, 3, channels, channels),
+        sums[second],
+        sums[first:second],
     )
 
 

time: 189 us -> 112 us (0.59)
  waiting for transfers between devices: 73.3 us -> 0 us
  Pallas kernels: 63.7 us -> 103 us
  blocking collectives: 31.8 us -> 0 us
  between operations: 14.1 us -> 0.66 us
    psum x1 -> x0, waiting for transfers between devices: 73.2 us -> none  [per_device(): lax.psum((conv_grad, bias_grad, proj_grad), 'rows')]
    pallas_call x0 -> x1, Pallas kernels: none -> 39.6 us  [reduce_sums(): pl.pallas_call(functools.partial(reduce_kernel, size), out_shape=jax.Shap...]
    psum x1 -> x0, blocking collectives: 31.8 us -> none  [per_device(): lax.psum((conv_grad, bias_grad, proj_grad), 'rows')]
    slice x0 -> x3, local copies, waits for them, and re-layouts: none -> 5.87 us  [the longest x1 2.86 us: per_device(): sums[:first].reshape(3, 3, channels, channels)]
    unnamed x6 -> x0, local copies, waits for them, and re-layouts: 4.73 us -> none
  transfers between devices with their start and end apart: 1 -> 0, of which waited for: 1 -> 0; matrix products, arithmetic and copies ran while one was open for 0% -> 0% of each run, Pallas kernels for 0% -> 0%
where the time goes in v1:
time: 112 us; the launch traced here: 111 us
  Pallas kernels  103 us (92%)
  local copies, waits for them, and re-layouts  5.87 us (5%)
  other arithmetic  1.68 us (2%)
    pallas_call x1, Pallas kernels, reduce_sums(): pl.pallas_call(functools.partial(reduce_kernel, size), out_shape=jax.Shap...  39.6 us
    pallas_call x1, Pallas kernels, coarse(): pl.pallas_call(functools.partial(coarse_kernel, left), out_shape=[jax.Sha...  17.6 us
    pallas_call x1, Pallas kernels, scatter(): pl.pallas_call(functools.partial(scatter_kernel, size, units), out_shape=...  17 us
    pallas_call x1, Pallas kernels, fine(): pl.pallas_call(functools.partial(fine_kernel, size, lead), grid=(fine_row...  16.6 us
    pallas_call x1, Pallas kernels, gather(): pl.pallas_call(functools.partial(gather_kernel, size, left, width), out_s...  12.3 us
    slice x1, local copies, waits for them, and re-layouts, per_device(): sums[:first].reshape(3, 3, channels, channels)  2.86 us

profile of v1, /device:TPU:0, one launch (start us, length us, event | category | flops | bytes accessed | tf_op | source)
XLA Modules:
  0.0 111.5 jit_solution(8218748879081719847)
XLA Ops:
  0.7 0.7 add_convert_fusion.1.blend_t
  1.3 1.0 add_convert_fusion.blend
  2.3 12.3 %shard_map.110 = (bf16[2,256,256]{2,1,0:T(8,128)(2,1)}, bf16[2,256,256]{2,1,0:T(8,128)(2,1)}, bf16[1,256,256]{2,1,0:T(8,128)(2,1)}, bf16[1,256,256]{2,1,0:T(8,128)(2,1)}, bf16[6,96,256]{2,1,0:T(8,128)(2,1)}) custom-call(bf16[8,256,256]{2,1,0:T(8,128)(2,1)} %ctx.3, bf16[8,256,256]{2,1,0:T(8,128)(2,1)} %cot.5), custom_call_target="tpu_custom_call" | custom-call | tf_op jit(solution)/shard_map/pallas_call | solution.py:133
  14.7 16.6 %shard_map.111 = (bf16[16,512,256]{2,1,0:T(8,128)(2,1)}, f32[512,256]{1,0:T(8,128)}, f32[4,64,256]{2,1,0:T(8,128)}) custom-call(bf16[6,96,256]{2,1,0:T(8,128)(2,1)} %get-tuple-element.16.crop_ctx, bf16[3,3,256,256]{3,2,1,0:T(8,128)(2,1)} %conv_w.3, f32[1,256]{1,0:T(1,128)} %bitcast.8, bf16[512,256]{1,0:T(8,128)(2,1)} %proj.1, ...), custom_call_target="tpu_custom_call" | custom-call | tf_op jit(solution)/shard_map/pallas_call | solution.py:252
  31.3 17.0 %shard_map.112 = bf16[6,2,64,256]{3,2,1,0:T(8,128)(2,1)} custom-call(f32[4,64,256]{2,1,0:T(8,128)} %get-tuple-element.22.parts), custom_call_target="tpu_custom_call" | custom-call | tf_op jit(solution)/shard_map/pallas_call | solution.py:349
  48.3 17.6 %shard_map.113 = (f32[8,256,256]{2,1,0:T(8,128)}, f32[9,256,256]{2,1,0:T(8,128)}, f32[8,256]{1,0:T(8,128)}) custom-call(bf16[8,256,256]{2,1,0:T(8,128)(2,1)} %ctx.3, bf16[2,256,256]{2,1,0:T(8,128)(2,1)} %get-tuple-element.18.c_top, bf16[2,256,256]{2,1,0:T(8,128)(2,1)} %get-tuple-element.19.c_bot, bf16[8,256,256]{2,1,0:T(8,128)(2,1)} %cot.5, ...), custom_call_target="tpu_custom_call" | custom-call | tf_op jit(solution)/shard_map/pallas_call | solution.py:453
  66.0 39.6 %shard_map.114 = bf16[3072,256]{1,0:T(8,128)(2,1)} custom-call(f32[2304,256]{1,0:T(8,128)} %bitcast.6, f32[512,256]{1,0:T(8,128)} %get-tuple-element.25.proj, f32[8,256]{1,0:T(8,128)} %get-tuple-element.26.bias), custom_call_target="tpu_custom_call" | custom-call | tf_op jit(solution)/shard_map/pallas_call | solution.py:587
  105.6 1.2 %slice.13 = f32[1,256]{1,0:T(1,128)} slice(bf16[3072,256]{1,0:T(8,128)(2,1)} %shard_map.114), slice={[2816:2817], [0:256]} | slice | bytes 2048 | tf_op jit(solution)/shard_map/slice | solution.py:627
  106.9 1.8 %slice.14 = f32[512,256]{1,0:T(8,128)} slice(bf16[3072,256]{1,0:T(8,128)(2,1)} %shard_map.114), slice={[2304:2816], [0:256]} | slice | bytes 1048576 | tf_op jit(solution)/shard_map/slice | solution.py:628
  108.6 2.9 %slice.12 = f32[2304,256]{1,0:T(8,128)} slice(bf16[3072,256]{1,0:T(8,128)(2,1)} %shard_map.114), slice={[0:2304], [0:256]} | slice | bytes 4718592 | tf_op jit(solution)/shard_map/slice | solution.py:626
  (2 shorter events, 0.0 us)

commit v2 on v1

--- a/solution.py
+++ b/solution.py
@@ -2,6 +2,7 @@
 
 import jax
 import jax.numpy as jnp
+import numpy as np
 from jax import lax
 from jax.experimental import pallas as pl
 from jax.experimental.pallas import tpu as pltpu
@@ -239,14 +240,14 @@
 def fine(size, lead, crop_ctx, conv_weight, conv_bias, proj_weight, hr, cot):
     fine_rows, cols, channels = hr.shape
     narrow = cols // 8
-    index = 2 * jnp.arange(cols, dtype=jnp.int32) - 7
-    lower = jnp.floor_divide(index, 16)
-    frac = (index - 16 * lower).astype(F32) / 16.0
-    column = jnp.arange(narrow, dtype=jnp.int32)[None, :]
-    left = jnp.clip(lower, 0, narrow - 1)[:, None]
-    right = jnp.clip(lower + 1, 0, narrow - 1)[:, None]
-    blend = (1.0 - frac)[:, None] * (column == left).astype(F32)
-    blend = (blend + frac[:, None] * (column == right).astype(F32)).astype(BF)
+    index = 2 * np.arange(cols) - 7
+    lower = index // 16
+    frac = ((index - 16 * lower) / 16.0)[:, None]
+    column = np.arange(narrow)[None, :]
+    left = np.clip(lower, 0, narrow - 1)[:, None]
+    right = np.clip(lower + 1, 0, narrow - 1)[:, None]
+    blend = (1.0 - frac) * (column == left) + frac * (column == right)
+    blend, blend_t = jnp.asarray(blend, BF), jnp.asarray(blend.T, BF)
     whole = lambda shape: pl.BlockSpec(shape, lambda s: (0,) * len(shape))
     tile = pl.BlockSpec((4, cols, channels), lambda s: (s, 0, 0))
     return pl.pallas_call(
@@ -274,10 +275,12 @@
             pltpu.VMEM((4, cols, channels), F32),
         ],
         compiler_params=pltpu.CompilerParams(vmem_limit_bytes=VMEM_LIMIT),
-    )(crop_ctx, conv_weight, conv_bias.reshape(1, -1), proj_weight, blend, blend.T, hr, cot)
-
-
-def scatter_kernel(size, units, parts, out, up, down, got_up, got_down, mine, send, recv, edge):
+    )(crop_ctx, conv_weight, conv_bias.reshape(1, -1), proj_weight, blend, blend_t, hr, cot)
+
+
+def scatter_kernel(
+    size, units, parts, ctx, c_top, c_bot, conv_w, bias, out, slope, ext, up, down, got_up, got_down, mine, send, recv, edge,
+):
     group, me = enter(size)
     base = 3 * size // 2
 
@@ -306,6 +309,32 @@
     @pl.when(me == size - 1)
     def _():
         got_down[...] = jnp.zeros_like(got_down)
+
+    rows, cols, channels = ctx.shape
+    ext[pl.ds(0, 2)] = c_top[...]
+    ext[pl.ds(2, rows)] = ctx[...]
+    ext[pl.ds(rows + 2, 2)] = c_bot[...]
+    column = lax.broadcasted_iota(jnp.int32, (cols, channels), 0)
+
+    def forward(p, carry):
+        sums = []
+        for b in range(3):
+            total = None
+            for a in range(3):
+                term = dot(ext[pl.ds(2 * p + a, 2)].reshape(2 * cols, channels), conv_w[a, b])
+                total = term if total is None else total + term
+            sums.append(total)
+        for k in range(2):
+            cut = slice(k * cols, (k + 1) * cols)
+            v = bias[...] + jnp.where(column == 0, 0.0, pltpu.roll(sums[0][cut], 1, 0))
+            v = v + sums[1][cut]
+            v = v + jnp.where(column == cols - 1, 0.0, pltpu.roll(sums[2][cut], cols - 1, 0))
+            s = sigmoid(v)
+            slope[2 * p + k] = s * (1.0 + v * (1.0 - s))
+        return carry
+
+    pairs = (rows + 2) // 2
+    lax.fori_loop(0, pairs - 2, forward, 0)
 
     for s in range(units + 2):
         index = units * me + s - 1 - base
@@ -333,6 +362,7 @@
         def _():
             out[s] = mine[...]
 
+    lax.fori_loop(pairs - 2, pairs, forward, 0)
     for s in range(units + 2):
         index = units * me + s - 1 - base
         here = (index >= 0) & (index < size) & (index != me)
@@ -343,15 +373,20 @@
     pl.when(has_down)(to_down.wait_send)
 
 
-def scatter(size, units, parts):
+def scatter(size, units, parts, context, c_top, c_bot, conv_weight, conv_bias):
+    rows, cols, _ = context.shape
     _, narrow, channels = parts.shape
     row = (narrow, channels)
     return pl.pallas_call(
         functools.partial(scatter_kernel, size, units),
-        out_shape=jax.ShapeDtypeStruct((units + 2, 2) + row, BF),
-        in_specs=[pl.BlockSpec(memory_space=pltpu.VMEM)],
-        out_specs=pl.BlockSpec(memory_space=pltpu.VMEM),
-        scratch_shapes=[pltpu.VMEM(row, BF)] * 4
+        out_shape=[
+            jax.ShapeDtypeStruct((units + 2, 2) + row, BF),
+            jax.ShapeDtypeStruct((rows + 2, cols, channels), F32),
+        ],
+        in_specs=[pl.BlockSpec(memory_space=pltpu.VMEM)] * 6,
+        out_specs=[pl.BlockSpec(memory_space=pltpu.VMEM)] * 2,
+        scratch_shapes=[pltpu.VMEM((rows + 4, cols, channels), BF)]
+        + [pltpu.VMEM(row, BF)] * 4
         + [
             pltpu.VMEM((2,) + row, BF),
             pltpu.SemaphoreType.DMA((units + 4,)),
@@ -361,11 +396,11 @@
         compiler_params=pltpu.CompilerParams(
             collective_id=1, has_side_effects=True, vmem_limit_bytes=VMEM_LIMIT
         ),
-    )(parts)
+    )(parts, context, c_top, c_bot, conv_weight, conv_bias.reshape(1, -1))
 
 
 def coarse_kernel(
-    left, ctx, c_top, c_bot, cot, g_top, g_bot, crop_grad, conv_w, bias,
+    left, ctx, c_top, c_bot, cot, g_top, g_bot, crop_grad, conv_w, slope,
     grad, wgrad, bgrad, ext, ext_t, outg, pre_g,
 ):
     rows, cols, channels = ctx.shape
@@ -393,29 +428,17 @@
     lax.fori_loop(0, rows + 2, turn, 0)
     bgrad[...] = jnp.zeros_like(bgrad)
 
-    def forward(p, carry):
-        sums = []
-        for b in range(3):
-            total = None
-            for a in range(3):
-                term = dot(ext[pl.ds(2 * p + a, 2)].reshape(2 * cols, channels), conv_w[a, b])
-                total = term if total is None else total + term
-            sums.append(total)
-        for k in range(2):
-            cut = slice(k * cols, (k + 1) * cols)
-            r = 2 * p + k
-            v = bias[...] + later(sums[0][cut]) + sums[1][cut] + sooner(sums[2][cut])
-            s = sigmoid(v)
-            g = (outg[r] * (s * (1.0 + v * (1.0 - s)))).astype(BF)
-            pre_g[1, r] = g
-            g = g.astype(F32)
-            pre_g[0, r] = sooner(g).astype(BF)
-            pre_g[2, r] = later(g).astype(BF)
-            own = ((r >= 1) & (r <= rows)).astype(F32)
-            bgrad[pl.ds(0, 1)] += own * jnp.sum(g, axis=0, keepdims=True)
-        return carry
-
-    lax.fori_loop(0, (rows + 2) // 2, forward, 0)
+    def forward(r, carry):
+        g = (outg[r] * slope[r]).astype(BF)
+        pre_g[1, r] = g
+        g = g.astype(F32)
+        pre_g[0, r] = sooner(g).astype(BF)
+        pre_g[2, r] = later(g).astype(BF)
+        own = ((r >= 1) & (r <= rows)).astype(F32)
+        bgrad[pl.ds(0, 1)] += own * jnp.sum(g, axis=0, keepdims=True)
+        return carry
+
+    lax.fori_loop(0, rows + 2, forward, 0)
 
     def backward(p, carry):
         sums = []
@@ -447,7 +470,7 @@
     lax.fori_loop(0, 9, weights, 0)
 
 
-def coarse(left, context, halos, cot_context, crop_grad, conv_weight, conv_bias):
+def coarse(left, context, halos, cot_context, crop_grad, conv_weight, slope):
     rows, cols, channels = context.shape
     c_top, c_bot, g_top, g_bot = halos
     return pl.pallas_call(
@@ -466,8 +489,7 @@
             pltpu.VMEM((3, rows + 2, cols, channels), BF),
         ],
         compiler_params=pltpu.CompilerParams(vmem_limit_bytes=VMEM_LIMIT),
-    )(context, c_top, c_bot, cot_context, g_top, g_bot, crop_grad, conv_weight,
-      conv_bias.reshape(1, -1))
+    )(context, c_top, c_bot, cot_context, g_top, g_bot, crop_grad, conv_weight, slope)
 
 
 def reduce_kernel(size, conv, proj, bias, out, acc, outgoing, incoming, send, recv, back, load):
@@ -604,6 +626,31 @@
     )(conv, proj, bias)
 
 
+def widen_kernel(sums, conv, proj, bias):
+    n_conv, n_proj = conv.shape[0], proj.shape[0]
+    step = 256
+
+    def body(n, carry):
+        at = pl.ds(pl.multiple_of(n * step, step), step)
+        conv[at] = sums[at].astype(F32)
+        return carry
+
+    lax.fori_loop(0, n_conv // step, body, 0)
+    proj[...] = sums[pl.ds(n_conv, n_proj)].astype(F32)
+    bias[...] = sums[pl.ds(n_conv + n_proj, 16)].astype(F32)[:1]
+
+
+def widen(sums):
+    channels = sums.shape[1]
+    return pl.pallas_call(
+        widen_kernel,
+        out_shape=[jax.ShapeDtypeStruct((n, channels), F32) for n in (9 * channels, 2 * channels, 1)],
+        in_specs=[pl.BlockSpec(memory_space=pltpu.VMEM)],
+        out_specs=[pl.BlockSpec(memory_space=pltpu.VMEM)] * 3,
+        compiler_params=pltpu.CompilerParams(vmem_limit_bytes=VMEM_LIMIT),
+    )(sums)
+
+
 def per_device(size, context, conv_weight, conv_bias, hr_features, proj_weight, cot_joined,
                cot_context):
     rows, cols, channels = context.shape
@@ -614,18 +661,22 @@
     joined, proj_grad, parts = fine(
         size, lead, crop_ctx, conv_weight, conv_bias, proj_weight, hr_features, cot_joined
     )
-    crop_grad = scatter(size, rows // 2, parts).reshape(-1, narrow, channels)
+    crop_grad, slope = scatter(
+        size, rows // 2, parts, context, *halos[:2], conv_weight, conv_bias
+    )
+    crop_grad = crop_grad.reshape(-1, narrow, channels)
     grad, conv_grad, bias_grad = coarse(
-        left, context, halos, cot_context, crop_grad, conv_weight, conv_bias
+        left, context, halos, cot_context, crop_grad, conv_weight, slope
     )
-    sums = reduce_sums(size, conv_grad.reshape(-1, channels), proj_grad, bias_grad).astype(F32)
-    first, second = 9 * channels, 11 * channels
+    conv_sum, proj_sum, bias_sum = widen(
+        reduce_sums(size, conv_grad.reshape(-1, channels), proj_grad, bias_grad)
+    )
     return (
         joined,
         grad,
-        sums[:first].reshape(3, 3, channels, channels),
-        sums[second],
-        sums[first:second],
+        conv_sum.reshape(3, 3, channels, channels),
+        bias_sum.reshape(-1),
+        proj_sum,
     )
 
 

time: 112 us -> 107 us (0.955)
  local copies, waits for them, and re-layouts: 5.87 us -> 0 us
  Pallas kernels: 103 us -> 106 us
  other arithmetic: 1.68 us -> 0 us
    slice x3 -> x0, local copies, waits for them, and re-layouts: 5.87 us -> none  [the longest x1 2.86 us: per_device(): sums[:first].reshape(3, 3, channels, channels)]
    pallas_call x1, Pallas kernels: 17 us -> 21.3 us  [scatter(): pl.pallas_call(functools.partial(scatter_kernel, size, units), out_shape=...]
    pallas_call x1, Pallas kernels: 17.6 us -> 14.1 us  [coarse(): pl.pallas_call(functools.partial(coarse_kernel, left), out_shape=[jax.Sha...]
    pallas_call x0 -> x1, Pallas kernels: none -> 3.15 us  [widen(): pl.pallas_call(widen_kernel, out_shape=[jax.ShapeDtypeStruct((n, channels...]
    convert_element_type x2 -> x0, other arithmetic: 1.65 us -> none  [fine(): blend = (blend + frac[:, None] * (column == right).astype(F32)).astype(BF)]
    pallas_call x1, Pallas kernels: 39.6 us -> 38.3 us  [reduce_sums(): pl.pallas_call(functools.partial(reduce_kernel, size), out_shape=jax.Shap...]
where the time goes in v2:
time: 107 us
  Pallas kernels  106 us (99%)
    pallas_call x1, Pallas kernels, reduce_sums(): pl.pallas_call(functools.partial(reduce_kernel, size), out_shape=jax.Shap...  38.3 us
    pallas_call x1, Pallas kernels, scatter(): pl.pallas_call(functools.partial(scatter_kernel, size, units), out_shape=...  21.3 us
    pallas_call x1, Pallas kernels, fine(): pl.pallas_call(functools.partial(fine_kernel, size, lead), grid=(fine_row...  16.6 us
    pallas_call x1, Pallas kernels, coarse(): pl.pallas_call(functools.partial(coarse_kernel, left), out_shape=[jax.Sha...  14.1 us
    pallas_call x1, Pallas kernels, gather(): pl.pallas_call(functools.partial(gather_kernel, size, left, width), out_s...  12.5 us
    pallas_call x1, Pallas kernels, widen(): pl.pallas_call(widen_kernel, out_shape=[jax.ShapeDtypeStruct((n, channels...  3.15 us

profile of v2, /device:TPU:0, one launch (start us, length us, event | category | flops | bytes accessed | tf_op | source)
XLA Modules:
  0.0 106.7 jit_solution(12051696677884524896)
XLA Ops:
  0.6 12.5 %shard_map.128 = (bf16[2,256,256]{2,1,0:T(8,128)(2,1)}, bf16[2,256,256]{2,1,0:T(8,128)(2,1)}, bf16[1,256,256]{2,1,0:T(8,128)(2,1)}, bf16[1,256,256]{2,1,0:T(8,128)(2,1)}, bf16[6,96,256]{2,1,0:T(8,128)(2,1)}) custom-call(bf16[8,256,256]{2,1,0:T(8,128)(2,1)} %ctx.5, bf16[8,256,256]{2,1,0:T(8,128)(2,1)} %cot.5), custom_call_target="tpu_custom_call" | custom-call | tf_op jit(solution)/shard_map/pallas_call | solution.py:134
  13.1 16.6 %shard_map.129 = (bf16[16,512,256]{2,1,0:T(8,128)(2,1)}, f32[512,256]{1,0:T(8,128)}, f32[4,64,256]{2,1,0:T(8,128)}) custom-call(bf16[6,96,256]{2,1,0:T(8,128)(2,1)} %get-tuple-element.21.crop_ctx, bf16[3,3,256,256]{3,2,1,0:T(8,128)(2,1)} %conv_w.5, f32[1,256]{1,0:T(1,128)} %bitcast.7, bf16[512,256]{1,0:T(8,128)(2,1)} %proj.1, ...), custom_call_target="tpu_custom_call" | custom-call | tf_op jit(solution)/shard_map/pallas_call | solution.py:253
  29.8 21.3 %shard_map.130 = (bf16[6,2,64,256]{3,2,1,0:T(8,128)(2,1)}, f32[10,256,256]{2,1,0:T(8,128)}) custom-call(f32[4,64,256]{2,1,0:T(8,128)} %get-tuple-element.27.parts, bf16[8,256,256]{2,1,0:T(8,128)(2,1)} %ctx.5, bf16[2,256,256]{2,1,0:T(8,128)(2,1)} %get-tuple-element.23.c_top, bf16[2,256,256]{2,1,0:T(8,128)(2,1)} %get-tuple-element.24.c_bot, ...), custom_call_target="tpu_custom_call" | custom-call | tf_op jit(solution)/shard_map/pallas_call | solution.py:380
  51.1 14.1 %shard_map.131 = (f32[8,256,256]{2,1,0:T(8,128)}, f32[9,256,256]{2,1,0:T(8,128)}, f32[8,256]{1,0:T(8,128)}) custom-call(bf16[8,256,256]{2,1,0:T(8,128)(2,1)} %ctx.5, bf16[2,256,256]{2,1,0:T(8,128)(2,1)} %get-tuple-element.23.c_top, bf16[2,256,256]{2,1,0:T(8,128)(2,1)} %get-tuple-element.24.c_bot, bf16[8,256,256]{2,1,0:T(8,128)(2,1)} %cot.5, ...), custom_call_target="tpu_custom_call" | custom-call | tf_op jit(solution)/shard_map/pallas_call | solution.py:476
  65.2 38.3 %shard_map.132.sums = bf16[3072,256]{1,0:T(8,128)(2,1)} custom-call(f32[2304,256]{1,0:T(8,128)} %bitcast.5, f32[512,256]{1,0:T(8,128)} %get-tuple-element.32.proj, f32[8,256]{1,0:T(8,128)} %get-tuple-element.33.bias), custom_call_target="tpu_custom_call" | custom-call | tf_op jit(solution)/shard_map/pallas_call | solution.py:609
  103.5 3.2 %shard_map.133 = (f32[2304,256]{1,0:T(8,128)}, f32[512,256]{1,0:T(8,128)}, f32[1,256]{1,0:T(1,128)}) custom-call(bf16[3072,256]{1,0:T(8,128)(2,1)} %shard_map.132.sums), custom_call_target="tpu_custom_call" | custom-call | tf_op jit(solution)/shard_map/pallas_call | solution.py:645

commit v3 on v2

--- a/solution.py
+++ b/solution.py
@@ -44,7 +44,7 @@
     return group, me
 
 
-def gather_kernel(size, left, width, ctx, cot, c_top, c_bot, g_top, g_bot, crop, send, recv, local):
+def gather_kernel(size, left, width, ctx, crop, send, recv, local):
     group, me = enter(size)
     rows = ctx.shape[0]
     units = rows // 2
@@ -91,26 +91,6 @@
                     near.wait()
 
     has_up, has_down = me > 0, me < size - 1
-    for ok, peer, src, dst, slot in (
-        (has_up, me - 1, ctx.at[pl.ds(0, 2)], c_bot, 3),
-        (has_down, me + 1, ctx.at[pl.ds(rows - 2, 2)], c_top, 4),
-        (has_up, me - 1, cot.at[pl.ds(0, 1)], g_bot, 5),
-        (has_down, me + 1, cot.at[pl.ds(rows - 1, 1)], g_top, 6),
-    ):
-        copy = remote(src, dst, len(sends), slot, peer)
-        sends.append((ok, copy))
-        pl.when(ok)(copy.start)
-
-    @pl.when(me == 0)
-    def _():
-        c_top[...] = jnp.zeros_like(c_top)
-        g_top[...] = jnp.zeros_like(g_top)
-
-    @pl.when(me == size - 1)
-    def _():
-        c_bot[...] = jnp.zeros_like(c_bot)
-        g_bot[...] = jnp.zeros_like(g_bot)
-
     mine = (base + me) // units
     take = remote(place(1), place(1), 0, 1, me)
     pl.when(mine != me)(take.wait_recv)
@@ -120,31 +100,26 @@
         pl.when(ok)(copy.start)
     for k in (0, 2):
         remote(place(k), place(k), 0, k, me).wait_recv()
-    pl.when(has_up)(remote(c_top, c_top, 0, 4, me).wait_recv)
-    pl.when(has_up)(remote(g_top, g_top, 0, 6, me).wait_recv)
-    pl.when(has_down)(remote(c_bot, c_bot, 0, 3, me).wait_recv)
-    pl.when(has_down)(remote(g_bot, g_bot, 0, 5, me).wait_recv)
     for ok, copy in sends:
         pl.when(ok)(copy.wait_send)
 
 
-def gather(size, context, cot_context, left, width):
-    rows, cols, channels = context.shape
-    shapes = [(2, cols, channels)] * 2 + [(1, cols, channels)] * 2 + [(6, width, channels)]
+def gather(size, context, left, width):
+    rows, _, channels = context.shape
     return pl.pallas_call(
         functools.partial(gather_kernel, size, left, width),
-        out_shape=[jax.ShapeDtypeStruct(shape, BF) for shape in shapes],
-        in_specs=[pl.BlockSpec(memory_space=pl.ANY)] * 2,
-        out_specs=[pl.BlockSpec(memory_space=pltpu.VMEM)] * 5,
+        out_shape=jax.ShapeDtypeStruct((6, width, channels), BF),
+        in_specs=[pl.BlockSpec(memory_space=pl.ANY)],
+        out_specs=pl.BlockSpec(memory_space=pltpu.VMEM),
         scratch_shapes=[
             pltpu.SemaphoreType.DMA((rows // 2 + 8,)),
-            pltpu.SemaphoreType.DMA((7,)),
+            pltpu.SemaphoreType.DMA((3,)),
             pltpu.SemaphoreType.DMA,
         ],
         compiler_params=pltpu.CompilerParams(
             collective_id=0, has_side_effects=True, vmem_limit_bytes=VMEM_LIMIT
         ),
-    )(context, cot_context)
+    )(context)
 
 
 def fine_kernel(
@@ -279,7 +254,8 @@
 
 
 def scatter_kernel(
-    size, units, parts, ctx, c_top, c_bot, conv_w, bias, out, slope, ext, up, down, got_up, got_down, mine, send, recv, edge,
+    size, units, parts, ctx, cot, conv_w, bias, out, slope, g_top, g_bot,
+    ext, up, down, got_up, got_down, mine, send, recv, edge, h_send, h_recv,
 ):
     group, me = enter(size)
     base = 3 * size // 2
@@ -311,9 +287,29 @@
         got_down[...] = jnp.zeros_like(got_down)
 
     rows, cols, channels = ctx.shape
-    ext[pl.ds(0, 2)] = c_top[...]
+    above, below = ext.at[pl.ds(0, 2)], ext.at[pl.ds(rows + 2, 2)]
+    halos = []
+    for n, (ok, peer, src, dst) in enumerate((
+        (has_up, me - 1, ctx.at[pl.ds(0, 2)], below),
+        (has_down, me + 1, ctx.at[pl.ds(rows - 2, 2)], above),
+        (has_up, me - 1, cot.at[pl.ds(0, 1)], g_bot),
+        (has_down, me + 1, cot.at[pl.ds(rows - 1, 1)], g_top),
+    )):
+        copy = remote(src, dst, h_send.at[n], h_recv.at[n], peer)
+        halos.append((ok, copy))
+        pl.when(ok)(copy.start)
+
+    @pl.when(me == 0)
+    def _():
+        ext[pl.ds(0, 2)] = jnp.zeros((2, cols, channels), BF)
+        g_top[...] = jnp.zeros_like(g_top)
+
+    @pl.when(me == size - 1)
+    def _():
+        ext[pl.ds(rows + 2, 2)] = jnp.zeros((2, cols, channels), BF)
+        g_bot[...] = jnp.zeros_like(g_bot)
+
     ext[pl.ds(2, rows)] = ctx[...]
-    ext[pl.ds(rows + 2, 2)] = c_bot[...]
     column = lax.broadcasted_iota(jnp.int32, (cols, channels), 0)
 
     def forward(p, carry):
@@ -334,7 +330,7 @@
         return carry
 
     pairs = (rows + 2) // 2
-    lax.fori_loop(0, pairs - 2, forward, 0)
+    lax.fori_loop(1, pairs - 1, forward, 0)
 
     for s in range(units + 2):
         index = units * me + s - 1 - base
@@ -362,7 +358,13 @@
         def _():
             out[s] = mine[...]
 
-    lax.fori_loop(pairs - 2, pairs, forward, 0)
+    for n, (ok, dst) in enumerate(
+        ((has_down, below), (has_up, above), (has_down, g_bot), (has_up, g_top))
+    ):
+        pl.when(ok)(remote(dst, dst, h_send.at[n], h_recv.at[n], me).wait_recv)
+    lax.fori_loop(0, 2, lambda n, carry: forward(n * (pairs - 1), carry), 0)
+    for ok, copy in halos:
+        pl.when(ok)(copy.wait_send)
     for s in range(units + 2):
         index = units * me + s - 1 - base
         here = (index >= 0) & (index < size) & (index != me)
@@ -373,7 +375,7 @@
     pl.when(has_down)(to_down.wait_send)
 
 
-def scatter(size, units, parts, context, c_top, c_bot, conv_weight, conv_bias):
+def scatter(size, units, parts, context, cot, conv_weight, conv_bias):
     rows, cols, _ = context.shape
     _, narrow, channels = parts.shape
     row = (narrow, channels)
@@ -382,32 +384,33 @@
         out_shape=[
             jax.ShapeDtypeStruct((units + 2, 2) + row, BF),
             jax.ShapeDtypeStruct((rows + 2, cols, channels), F32),
-        ],
-        in_specs=[pl.BlockSpec(memory_space=pltpu.VMEM)] * 6,
-        out_specs=[pl.BlockSpec(memory_space=pltpu.VMEM)] * 2,
-        scratch_shapes=[pltpu.VMEM((rows + 4, cols, channels), BF)]
-        + [pltpu.VMEM(row, BF)] * 4
+            jax.ShapeDtypeStruct((1, cols, channels), BF),
+            jax.ShapeDtypeStruct((1, cols, channels), BF),
+            jax.ShapeDtypeStruct((rows + 4, cols, channels), BF),
+        ],
+        in_specs=[pl.BlockSpec(memory_space=pltpu.VMEM)] * 5,
+        out_specs=[pl.BlockSpec(memory_space=pltpu.VMEM)] * 5,
+        scratch_shapes=[pltpu.VMEM(row, BF)] * 4
         + [
             pltpu.VMEM((2,) + row, BF),
             pltpu.SemaphoreType.DMA((units + 4,)),
             pltpu.SemaphoreType.DMA((units + 2,)),
             pltpu.SemaphoreType.DMA((2,)),
+            pltpu.SemaphoreType.DMA((4,)),
+            pltpu.SemaphoreType.DMA((4,)),
         ],
         compiler_params=pltpu.CompilerParams(
             collective_id=1, has_side_effects=True, vmem_limit_bytes=VMEM_LIMIT
         ),
-    )(parts, context, c_top, c_bot, conv_weight, conv_bias.reshape(1, -1))
+    )(parts, context, cot, conv_weight, conv_bias.reshape(1, -1))
 
 
 def coarse_kernel(
-    left, ctx, c_top, c_bot, cot, g_top, g_bot, crop_grad, conv_w, slope,
-    grad, wgrad, bgrad, ext, ext_t, outg, pre_g,
+    left, ext, cot, g_top, g_bot, crop_grad, conv_w, slope,
+    grad, wgrad, bgrad, ext_t, outg, pre_g,
 ):
-    rows, cols, channels = ctx.shape
+    rows, cols, channels = cot.shape
     narrow = crop_grad.shape[1]
-    ext[pl.ds(0, 2)] = c_top[...]
-    ext[pl.ds(2, rows)] = ctx[...]
-    ext[pl.ds(rows + 2, 2)] = c_bot[...]
     outg[pl.ds(0, 1)] = g_top[...].astype(F32)
     outg[pl.ds(1, rows)] = cot[...].astype(F32)
     outg[pl.ds(rows + 1, 1)] = g_bot[...].astype(F32)
@@ -470,9 +473,9 @@
     lax.fori_loop(0, 9, weights, 0)
 
 
-def coarse(left, context, halos, cot_context, crop_grad, conv_weight, slope):
-    rows, cols, channels = context.shape
-    c_top, c_bot, g_top, g_bot = halos
+def coarse(left, ext, edges, cot_context, crop_grad, conv_weight, slope):
+    rows, cols, channels = cot_context.shape
+    g_top, g_bot = edges
     return pl.pallas_call(
         functools.partial(coarse_kernel, left),
         out_shape=[
@@ -480,16 +483,15 @@
             jax.ShapeDtypeStruct((9, channels, channels), F32),
             jax.ShapeDtypeStruct((8, channels), F32),
         ],
-        in_specs=[pl.BlockSpec(memory_space=pltpu.VMEM)] * 9,
+        in_specs=[pl.BlockSpec(memory_space=pltpu.VMEM)] * 7,
         out_specs=[pl.BlockSpec(memory_space=pltpu.VMEM)] * 3,
         scratch_shapes=[
-            pltpu.VMEM((rows + 4, cols, channels), BF),
             pltpu.VMEM((rows + 2, channels, cols), BF),
             pltpu.VMEM((rows + 2, cols, channels), F32),
             pltpu.VMEM((3, rows + 2, cols, channels), BF),
         ],
         compiler_params=pltpu.CompilerParams(vmem_limit_bytes=VMEM_LIMIT),
-    )(context, c_top, c_bot, cot_context, g_top, g_bot, crop_grad, conv_weight, slope)
+    )(ext, cot_context, g_top, g_bot, crop_grad, conv_weight, slope)
 
 
 def reduce_kernel(size, conv, proj, bias, out, acc, outgoing, incoming, send, recv, back, load):
@@ -657,16 +659,16 @@
     narrow = hr_features.shape[1] // 8
     left = (cols - narrow) // 2
     lead = 16
-    *halos, crop_ctx = gather(size, context, cot_context, left - lead, narrow + 2 * lead)
+    crop_ctx = gather(size, context, left - lead, narrow + 2 * lead)
     joined, proj_grad, parts = fine(
         size, lead, crop_ctx, conv_weight, conv_bias, proj_weight, hr_features, cot_joined
     )
-    crop_grad, slope = scatter(
-        size, rows // 2, parts, context, *halos[:2], conv_weight, conv_bias
+    crop_grad, slope, *edges, ext = scatter(
+        size, rows // 2, parts, context, cot_context, conv_weight, conv_bias
     )
     crop_grad = crop_grad.reshape(-1, narrow, channels)
     grad, conv_grad, bias_grad = coarse(
-        left, context, halos, cot_context, crop_grad, conv_weight, slope
+        left, ext, edges, cot_context, crop_grad, conv_weight, slope
     )
     conv_sum, proj_sum, bias_sum = widen(
         reduce_sums(size, conv_grad.reshape(-1, channels), proj_grad, bias_grad)

time: 107 us -> 109 us (1.019)
  Pallas kernels: 106 us -> 109 us
    pallas_call x1, Pallas kernels: 38.3 us -> 45.1 us  [reduce_sums(): pl.pallas_call(functools.partial(reduce_kernel, size), out_shape=jax.Shap...]
    pallas_call x1, Pallas kernels: 21.3 us -> 17.6 us  [scatter(): pl.pallas_call(functools.partial(scatter_kernel, size, units), out_shape=...]
where the time goes in v3:
time: 109 us
  Pallas kernels  109 us (100%)
    pallas_call x1, Pallas kernels, reduce_sums(): pl.pallas_call(functools.partial(reduce_kernel, size), out_shape=jax.Shap...  45.1 us
    pallas_call x1, Pallas kernels, scatter(): pl.pallas_call(functools.partial(scatter_kernel, size, units), out_shape=...  17.6 us
    pallas_call x1, Pallas kernels, fine(): pl.pallas_call(functools.partial(fine_kernel, size, lead), grid=(fine_row...  16.6 us
    pallas_call x1, Pallas kernels, coarse(): pl.pallas_call(functools.partial(coarse_kernel, left), out_shape=[jax.Sha...  14 us
    pallas_call x1, Pallas kernels, gather(): pl.pallas_call(functools.partial(gather_kernel, size, left, width), out_s...  12 us
    pallas_call x1, Pallas kernels, widen(): pl.pallas_call(widen_kernel, out_shape=[jax.ShapeDtypeStruct((n, channels...  3.15 us

profile of v3, /device:TPU:0, one launch (start us, length us, event | category | flops | bytes accessed | tf_op | source)
XLA Modules:
  0.0 109.2 jit_solution(11243874407115899926)
XLA Ops:
  0.6 12.0 %shard_map.128.crop_ctx = bf16[6,96,256]{2,1,0:T(8,128)(2,1)} custom-call(bf16[8,256,256]{2,1,0:T(8,128)(2,1)} %ctx.3), custom_call_target="tpu_custom_call" | custom-call | tf_op jit(solution)/shard_map/pallas_call | solution.py:109
  12.7 16.6 %shard_map.129 = (bf16[16,512,256]{2,1,0:T(8,128)(2,1)}, f32[512,256]{1,0:T(8,128)}, f32[4,64,256]{2,1,0:T(8,128)}) custom-call(bf16[6,96,256]{2,1,0:T(8,128)(2,1)} %shard_map.128.crop_ctx, bf16[3,3,256,256]{3,2,1,0:T(8,128)(2,1)} %conv_w.5, f32[1,256]{1,0:T(1,128)} %bitcast.7, bf16[512,256]{1,0:T(8,128)(2,1)} %proj.1, bf16[512,64]{1,0:T(8,128)(2,1)} %constant.4.clone.blend, ...), custom_call_target="tpu_custom_call" | custom-call | tf_op jit(solution)/shard_map/pallas_call | solution.py:228
  29.3 17.6 %shard_map.130 = (bf16[6,2,64,256]{3,2,1,0:T(8,128)(2,1)}, f32[10,256,256]{2,1,0:T(8,128)}, bf16[1,256,256]{2,1,0:T(8,128)(2,1)}, bf16[1,256,256]{2,1,0:T(8,128)(2,1)}, bf16[12,256,256]{2,1,0:T(8,128)(2,1)}) custom-call(f32[4,64,256]{2,1,0:T(8,128)} %get-tuple-element.20.parts, bf16[8,256,256]{2,1,0:T(8,128)(2,1)} %ctx.3, bf16[8,256,256]{2,1,0:T(8,128)(2,1)} %cot.5, ...), custom_call_target="tpu_custom_call" | custom-call | tf_op jit(solution)/shard_map/pallas_call | solution.py:382
  46.9 14.0 %shard_map.131 = (f32[8,256,256]{2,1,0:T(8,128)}, f32[9,256,256]{2,1,0:T(8,128)}, f32[8,256]{1,0:T(8,128)}) custom-call(bf16[12,256,256]{2,1,0:T(8,128)(2,1)} %get-tuple-element.21.ext, bf16[8,256,256]{2,1,0:T(8,128)(2,1)} %cot.5, bf16[1,256,256]{2,1,0:T(8,128)(2,1)} %get-tuple-element.22.g_top, bf16[1,256,256]{2,1,0:T(8,128)(2,1)} %get-tuple-element.23.g_bot, ...), custom_call_target="tpu_custom_call" | custom-call | tf_op jit(solution)/shard_map/pallas_call | solution.py:479
  61.0 45.1 %shard_map.132.sums = bf16[3072,256]{1,0:T(8,128)(2,1)} custom-call(f32[2304,256]{1,0:T(8,128)} %bitcast.5, f32[512,256]{1,0:T(8,128)} %get-tuple-element.28.proj, f32[8,256]{1,0:T(8,128)} %get-tuple-element.29.bias), custom_call_target="tpu_custom_call" | custom-call | tf_op jit(solution)/shard_map/pallas_call | solution.py:611
  106.1 3.2 %shard_map.133 = (f32[2304,256]{1,0:T(8,128)}, f32[512,256]{1,0:T(8,128)}, f32[1,256]{1,0:T(1,128)}) custom-call(bf16[3072,256]{1,0:T(8,128)(2,1)} %shard_map.132.sums), custom_call_target="tpu_custom_call" | custom-call | tf_op jit(solution)/shard_map/pallas_call | solution.py:647

commit v4 on v2

--- a/solution.py
+++ b/solution.py
@@ -156,7 +156,7 @@
     channels = hr.shape[2]
     cols = hr.shape[1]
     narrow, wide = blend.shape[1], crop_ctx.shape[1]
-    chunk = 128
+    chunk = 256
 
     @pl.when(step == 0)
     def _():

time: 107 us -> 104 us (0.972)
  Pallas kernels: 106 us -> 103 us
    pallas_call x1, Pallas kernels: 16.6 us -> 14.1 us  [fine(): pl.pallas_call(functools.partial(fine_kernel, size, lead), grid=(fine_row...]
where the time goes in v4:
time: 104 us
  Pallas kernels  103 us (99%)
    pallas_call x1, Pallas kernels, reduce_sums(): pl.pallas_call(functools.partial(reduce_kernel, size), out_shape=jax.Shap...  38.3 us
    pallas_call x1, Pallas kernels, scatter(): pl.pallas_call(functools.partial(scatter_kernel, size, units), out_shape=...  21.3 us
    pallas_call x1, Pallas kernels, coarse(): pl.pallas_call(functools.partial(coarse_kernel, left), out_shape=[jax.Sha...  14.1 us
    pallas_call x1, Pallas kernels, fine(): pl.pallas_call(functools.partial(fine_kernel, size, lead), grid=(fine_row...  14.1 us
    pallas_call x1, Pallas kernels, gather(): pl.pallas_call(functools.partial(gather_kernel, size, left, width), out_s...  12.5 us
    pallas_call x1, Pallas kernels, widen(): pl.pallas_call(widen_kernel, out_shape=[jax.ShapeDtypeStruct((n, channels...  3.15 us

profile of v4, /device:TPU:0, one launch (start us, length us, event | category | flops | bytes accessed | tf_op | source)
XLA Modules:
  0.0 104.1 jit_solution(1337627636943376600)
XLA Ops:
  0.6 12.5 %shard_map.128 = (bf16[2,256,256]{2,1,0:T(8,128)(2,1)}, bf16[2,256,256]{2,1,0:T(8,128)(2,1)}, bf16[1,256,256]{2,1,0:T(8,128)(2,1)}, bf16[1,256,256]{2,1,0:T(8,128)(2,1)}, bf16[6,96,256]{2,1,0:T(8,128)(2,1)}) custom-call(bf16[8,256,256]{2,1,0:T(8,128)(2,1)} %ctx.5, bf16[8,256,256]{2,1,0:T(8,128)(2,1)} %cot.5), custom_call_target="tpu_custom_call" | custom-call | tf_op jit(solution)/shard_map/pallas_call | solution.py:134
  13.1 14.1 %shard_map.129 = (bf16[16,512,256]{2,1,0:T(8,128)(2,1)}, f32[512,256]{1,0:T(8,128)}, f32[4,64,256]{2,1,0:T(8,128)}) custom-call(bf16[6,96,256]{2,1,0:T(8,128)(2,1)} %get-tuple-element.21.crop_ctx, bf16[3,3,256,256]{3,2,1,0:T(8,128)(2,1)} %conv_w.5, f32[1,256]{1,0:T(1,128)} %bitcast.7, bf16[512,256]{1,0:T(8,128)(2,1)} %proj.1, ...), custom_call_target="tpu_custom_call" | custom-call | tf_op jit(solution)/shard_map/pallas_call | solution.py:253
  27.2 21.3 %shard_map.130 = (bf16[6,2,64,256]{3,2,1,0:T(8,128)(2,1)}, f32[10,256,256]{2,1,0:T(8,128)}) custom-call(f32[4,64,256]{2,1,0:T(8,128)} %get-tuple-element.27.parts, bf16[8,256,256]{2,1,0:T(8,128)(2,1)} %ctx.5, bf16[2,256,256]{2,1,0:T(8,128)(2,1)} %get-tuple-element.23.c_top, bf16[2,256,256]{2,1,0:T(8,128)(2,1)} %get-tuple-element.24.c_bot, ...), custom_call_target="tpu_custom_call" | custom-call | tf_op jit(solution)/shard_map/pallas_call | solution.py:380
  48.5 14.1 %shard_map.131 = (f32[8,256,256]{2,1,0:T(8,128)}, f32[9,256,256]{2,1,0:T(8,128)}, f32[8,256]{1,0:T(8,128)}) custom-call(bf16[8,256,256]{2,1,0:T(8,128)(2,1)} %ctx.5, bf16[2,256,256]{2,1,0:T(8,128)(2,1)} %get-tuple-element.23.c_top, bf16[2,256,256]{2,1,0:T(8,128)(2,1)} %get-tuple-element.24.c_bot, bf16[8,256,256]{2,1,0:T(8,128)(2,1)} %cot.5, ...), custom_call_target="tpu_custom_call" | custom-call | tf_op jit(solution)/shard_map/pallas_call | solution.py:476
  62.7 38.3 %shard_map.132.sums = bf16[3072,256]{1,0:T(8,128)(2,1)} custom-call(f32[2304,256]{1,0:T(8,128)} %bitcast.5, f32[512,256]{1,0:T(8,128)} %get-tuple-element.32.proj, f32[8,256]{1,0:T(8,128)} %get-tuple-element.33.bias), custom_call_target="tpu_custom_call" | custom-call | tf_op jit(solution)/shard_map/pallas_call | solution.py:609
  101.0 3.2 %shard_map.133 = (f32[2304,256]{1,0:T(8,128)}, f32[512,256]{1,0:T(8,128)}, f32[1,256]{1,0:T(1,128)}) custom-call(bf16[3072,256]{1,0:T(8,128)(2,1)} %shard_map.132.sums), custom_call_target="tpu_custom_call" | custom-call | tf_op jit(solution)/shard_map/pallas_call | solution.py:645
